TPU v7x, 512 devices: a whole 4x4x16 slice. The times are simulated.
512 devices in a mesh: dp: 32 (over y, z_lo), tp: 16 (over z_hi, x, core).
Axes of the slice: x: 4, y: 4, z: 16 (z_hi: 2, z_lo: 8; z = z_hi * 8 + z_lo), core: 2. Of those that a mesh axis runs over, the one named last changes fastest.
Arguments:
- clean_latents: bfloat16 [32, 256, 3072], P('dp'), may hold values from -6 to 6
- noise: bfloat16 [32, 256, 3072], P('dp'), may hold values from -6 to 6
- time_index: int32 [32], P('dp'), may hold values from 0 to 999
- teacher_weights: bfloat16 [3072, 8192], P('dp', 'tp'), may hold values from -16 to 16, as said below
- student_weights: bfloat16 [3072, 8192], P('dp', 'tp'), may hold values from -16 to 16, as said below
- teacher_time: bfloat16 [256, 2048], P(None, 'tp'), may hold values from -0.375 to 0.375
- student_time: bfloat16 [256, 2048], P(None, 'tp'), may hold values from -0.375 to 0.375
Outputs:
- student_velocity: bfloat16 [32, 256, 3072], P('dp', 'tp')
- student_grad: bfloat16 [3072, 8192], P('dp', 'tp')
Inputs may be any that keep to these rules, and one draw needn't show every extreme that they name: `teacher_weights`: packed attention weights, per head query, key, value and output blocks. `student_weights`: packed attention weights, per head query, key, value and output blocks.
All inputs are finite; a program needn't handle non-finite values.
Results may differ from a plain program's by a relative error of at most 0.033.
Values may be sent and summed in bfloat16 or wider, within the bound.
A program may use at most 128 MiB of HBM per device.

v0:
```python
import math

import jax
import jax.numpy as jnp
from jax import lax
from jax.sharding import PartitionSpec as P

D = 3072
STEPS = 1000


def plan_time(time_step):
    return 0.05 + 1.45 * (time_step.astype(jnp.float32) + 0.5) / STEPS


def time_embedding(step_time, width):
    half_width = width // 2
    position = jnp.arange(half_width, dtype=jnp.float32)
    frequencies = 4.0 * jnp.exp(-jnp.log(100.0) * position / half_width)
    phases = step_time * frequencies
    time_features = jnp.concatenate([jnp.cos(phases), jnp.sin(phases)])
    time_slope = jnp.concatenate([-frequencies * jnp.sin(phases), frequencies * jnp.cos(phases)])
    return (time_features, time_slope)


def head_forward(normed_b, weight_block, gate_vec):
    head_size = weight_block.shape[1] // 4
    score_scale = head_size ** (-0.5)
    projections = jnp.dot(
        normed_b, weight_block[:, : 3 * head_size], preferred_element_type=jnp.float32
    ).astype(jnp.bfloat16)
    queries = projections[:, :head_size]
    key_rows = projections[:, head_size : 2 * head_size]
    values = projections[:, 2 * head_size :]
    scores = jnp.dot(queries, key_rows.T, preferred_element_type=jnp.float32) * score_scale
    attention = jax.nn.softmax(scores, axis=-1)
    attention_b = attention.astype(jnp.bfloat16)
    attended = jnp.dot(attention_b, values, preferred_element_type=jnp.float32)
    gated = (attended * (1.0 + gate_vec)).astype(jnp.bfloat16)
    head_term = jnp.dot(
        gated, weight_block[:, 3 * head_size :].T, preferred_element_type=jnp.float32
    )
    return (head_term, (queries, key_rows, values, attention, attention_b, attended, gated))


def head_tangent(d_normed_b, weight_block, gate_vec, gate_slope, stashed):
    queries, key_rows, values, attention, attention_b, attended, gated = stashed
    head_size = weight_block.shape[1] // 4
    score_scale = head_size ** (-0.5)
    d_proj = jnp.dot(
        d_normed_b, weight_block[:, : 3 * head_size], preferred_element_type=jnp.float32
    ).astype(jnp.bfloat16)
    d_queries = d_proj[:, :head_size]
    d_keys = d_proj[:, head_size : 2 * head_size]
    d_values = d_proj[:, 2 * head_size :]
    d_scores = (
        jnp.dot(d_queries, key_rows.T, preferred_element_type=jnp.float32)
        + jnp.dot(queries, d_keys.T, preferred_element_type=jnp.float32)
    ) * score_scale
    d_attention = attention * (d_scores - jnp.sum(attention * d_scores, axis=-1, keepdims=True))
    d_attention_b = d_attention.astype(jnp.bfloat16)
    d_attended = jnp.dot(d_attention_b, values, preferred_element_type=jnp.float32) + jnp.dot(
        attention_b, d_values, preferred_element_type=jnp.float32
    )
    d_gated = (d_attended * (1.0 + gate_vec) + attended * gate_slope).astype(jnp.bfloat16)
    return jnp.dot(d_gated, weight_block[:, 3 * head_size :].T, preferred_element_type=jnp.float32)


def head_backward(normed_b, cotangent_b, weight_block, gate_vec, stashed):
    queries, key_rows, values, attention, attention_b, attended, gated = stashed
    head_size = weight_block.shape[1] // 4
    score_scale = head_size ** (-0.5)
    grad_out = jnp.dot(cotangent_b.T, gated, preferred_element_type=jnp.float32)
    d_gated = jnp.dot(
        cotangent_b, weight_block[:, 3 * head_size :], preferred_element_type=jnp.float32
    )
    d_att_b = (d_gated * (1.0 + gate_vec)).astype(jnp.bfloat16)
    grad_values = jnp.dot(attention_b.T, d_att_b, preferred_element_type=jnp.float32)
    d_back = jnp.dot(d_att_b, values.T, preferred_element_type=jnp.float32)
    d_scores_b = (
        attention * (d_back - jnp.sum(attention * d_back, axis=-1, keepdims=True)) * score_scale
    ).astype(jnp.bfloat16)
    grad_queries = jnp.dot(d_scores_b, key_rows, preferred_element_type=jnp.float32)
    grad_keys = jnp.dot(d_scores_b.T, queries, preferred_element_type=jnp.float32)
    d_proj_b = jnp.concatenate([grad_queries, grad_keys, grad_values], axis=1).astype(jnp.bfloat16)
    grad_proj = jnp.dot(normed_b.T, d_proj_b, preferred_element_type=jnp.float32)
    return jnp.concatenate([grad_proj, grad_out], axis=1)


def on_device(
    clean_latents, noise, time_index, teacher_weights, student_weights, teacher_time, student_time
):
    step_time = plan_time(time_index[0])
    cosine = jnp.cos(step_time)
    sine = jnp.sin(step_time)
    noisy = cosine * clean_latents[0].astype(jnp.float32) + sine * noise[0].astype(jnp.float32)
    inv_rms = lax.rsqrt(jnp.mean(noisy * noisy, axis=-1, keepdims=True) + 1e-06)
    normed = noisy * inv_rms
    normed_b = normed.astype(jnp.bfloat16)
    time_features, time_slope = time_embedding(step_time, teacher_time.shape[0])
    teacher_full, student_full = (
        lax.all_gather(teacher_weights, "dp", axis=0, tiled=True),
        lax.all_gather(student_weights, "dp", axis=0, tiled=True),
    )
    teacher_gate = jnp.dot(
        time_features, teacher_time.astype(jnp.float32), precision=lax.Precision.HIGHEST
    )
    teacher_term = head_forward(normed_b, teacher_full, teacher_gate)[0]
    own_rows = noisy.shape[0] // lax.axis_size("tp")
    first_row = lax.axis_index("tp") * own_rows
    factor = math.sqrt(D / lax.axis_size("dp"))
    teacher_total = lax.psum(teacher_term.astype(jnp.bfloat16), "tp").astype(jnp.float32)
    velocity = (noisy + teacher_total).astype(jnp.bfloat16)
    table_f = student_time.astype(jnp.float32)
    student_gate = jnp.dot(time_features, table_f, precision=lax.Precision.HIGHEST)
    student_slope = jnp.dot(time_slope, table_f, precision=lax.Precision.HIGHEST)
    student_term, stashed = head_forward(normed_b, student_full, student_gate)
    tangent = velocity.astype(jnp.float32)
    d_normed = inv_rms * (tangent - normed * jnp.mean(normed * tangent, axis=-1, keepdims=True))
    d_normed_b = d_normed.astype(jnp.bfloat16)
    d_term = head_tangent(d_normed_b, student_full, student_gate, student_slope, stashed)
    term_total, d_total = (
        lax.psum(student_term.astype(jnp.bfloat16), "tp").astype(jnp.float32),
        lax.psum(d_term.astype(jnp.bfloat16), "tp").astype(jnp.float32),
    )
    predicted = noisy + term_total
    d_predicted = tangent + d_total
    target_gap = -(cosine * cosine) * (predicted - tangent) - cosine * sine * (noisy + d_predicted)
    gap_norm = jnp.sqrt(jnp.sum(target_gap * target_gap))
    cotangent_b = (target_gap * (-factor / (gap_norm + 0.1))).astype(jnp.bfloat16)
    own_out = lax.dynamic_slice_in_dim(predicted, first_row, own_rows, 0).astype(jnp.bfloat16)
    grad_block = head_backward(normed_b, cotangent_b, student_full, student_gate, stashed)
    gradients = lax.psum_scatter(
        grad_block.astype(jnp.bfloat16), "dp", scatter_dimension=0, tiled=True
    )
    return (own_out[None], gradients)


def solution(mesh):
    placed = (
        P("dp", None, None),
        P("dp", None, None),
        P("dp"),
        P("dp", "tp"),
        P("dp", "tp"),
        P(None, "tp"),
        P(None, "tp"),
    )
    return jax.shard_map(
        on_device,
        mesh=mesh,
        in_specs=placed,
        out_specs=(P("dp", "tp", None), P("dp", "tp")),
        check_vma=False,
    )
```

profile of v0, /device:TPU:2, one launch (start us, length us, event | category | flops | bytes accessed | tf_op | source)
XLA Modules:
  0.0 1328.1 jit_solution(3640644256411107830)
XLA Ops:
  7.3 0.7 all-gather.5.cloned.1.call-update
  8.0 0.7 all-gather.3.cloned.1.call-update
  9.7 2.7 fusion.7
  12.5 1.8 fusion.9
  14.4 232.9 %all-gather.5.cloned.1.call-done = bf16[3072,512]{1,0:T(8,128)(2,1)} async-done(((bf16[96,512]{1,0:T(8,128)(2,1)}), bf16[3072,512]{1,0:T(8,128)(2,1)}) %all-gather.5.cloned.1.call-update) | async-done | bytes 3145744 | tf_op jit(solution)/shard_map/all_gather | solution.py:102
  247.2 3.1 fusion.22
  250.4 0.7 copy-done.12
  251.3 3.1 convolution_convert_fusion.2
  254.8 225.6 %all-gather.3.cloned.1.call-done = bf16[3072,512]{1,0:T(8,128)(2,1)} async-done(((bf16[96,512]{1,0:T(8,128)(2,1)}), bf16[3072,512]{1,0:T(8,128)(2,1)}) %all-gather.3.cloned.1.call-update) | async-done | bytes 3145744 | tf_op jit(solution)/shard_map/all_gather | solution.py:103
  480.3 3.1 fusion.19
  485.0 2.9 convolution_convert_fusion.3
  487.9 246.0 %all-reduce.4.cloned.1.call-done = bf16[256,3072]{1,0:T(8,128)(2,1)} async-done(((bf16[256,3072]{1,0:T(8,128)(2,1)}), bf16[256,3072]{1,0:T(8,128)(2,1)}) %all-reduce.4.cloned.1.call-update) | async-done | bytes 1572880 | tf_op jit(solution)/shard_map/psum | solution.py:112
  733.9 2.7 fusion.2
  736.7 1.5 fusion.25
  738.9 0.9 fusion.50
  739.8 3.2 convolution_convert_fusion.1
  743.3 303.2 %all-reduce.6.cloned.1.call-done = (bf16[256,3072]{1,0:T(8,128)(2,1)}, bf16[256,3072]{1,0:T(8,128)(2,1)}) async-done(((bf16[256,3072]{1,0:T(8,128)(2,1)}, bf16[256,3072]{1,0:T(8,128)(2,1)}), (bf16[256,3072]{1,0:T(8,128)(2,1)}, bf16[256,3072]{1,0:T(8,128)(2,1)})) %all-reduce.6.cloned.1.call-update) | async-done | bytes 3145744 | tf_op jit(solution)/shard_map/psum | solution.py:123
  1046.5 6.4 multiply_reduce_fusion
  1053.7 2.8 fusion.34
  1058.2 0.8 convolution_convert_fusion
  1059.0 1.9 pad_maximum_fusion
  1060.9 4.7 copy.11
  1065.6 2.2 bitcast_add_fusion.1
  1068.4 253.2 %reduce-scatter.4.cloned.1.call-done = bf16[96,512]{1,0:T(8,128)(2,1)} async-done(((bf16[3072,512]{1,0:T(8,128)(2,1)}), bf16[96,512]{1,0:T(8,128)(2,1)}) %reduce-scatter.4.cloned.1.call-update) | async-done | bytes 98320
  (60 shorter events, 5.9 us)
Async XLA Ops:
  7.2 247.3 %copy-start = (bf16[256,128]{1,0:T(8,128)(2,1)S(1)}, bf16[256,128]{1,0:T(8,128)(2,1)}, u32[]{:S(2)}) copy-start(bf16[256,128]{1,0:T(8,128)(2,1)} %param.13) | copy-start | bytes 196612
  7.2 5.3 copy-start.2
  7.2 5.3 copy-start.1
  7.2 5.2 copy-start.14
  7.2 240.0 %all-gather.5.cloned.1.call-start = ((), (), s32[]{:S(2)}) async-start(), calls=%async_computation.2 | async-start | bytes 3244032 | tf_op jit(solution)/shard_map/all_gather | solution.py:102
  7.9 472.4 %all-gather.3.cloned.1.call-start = ((), (), s32[]{:S(2)}) async-start(), calls=%async_computation.1 | async-start | bytes 3244032 | tf_op jit(solution)/shard_map/all_gather | solution.py:103
  8.7 725.2 %all-reduce.4.cloned.1.call-start = ((), (), s32[]{:S(2)}) async-start(), calls=%async_computation.3 | async-start | bytes 3145728 | tf_op jit(solution)/shard_map/psum | solution.py:112
  250.4 0.7 copy-start.12
  254.4 792.1 %all-reduce.6.cloned.1.call-start = ((), (), s32[]{:S(2)}) async-start(), calls=%async_computation.5 | async-start | bytes 6291456 | tf_op jit(solution)/shard_map/psum | solution.py:123
  483.5 0.7 copy-start.9
  484.4 0.6 copy-start.7
  733.8 2.7 copy-start.5
  733.9 2.8 copy-start.6
  736.7 1.5 copy-start.10
  738.2 0.7 copy-start.13
  743.0 578.6 %reduce-scatter.4.cloned.1.call-start = ((), (), s32[]{:S(2)}) async-start(), calls=%async_computation.4 | async-start | bytes 3244032
  1053.7 2.8 copy-start.11
  1053.7 3.7 copy-start.3
  1053.7 3.7 copy-start.8
  1056.7 1.5 copy-start.4
Sparse Core Ops, SparseCore 0:
  10.1 237.0 all-gather.4
  249.3 230.9 all-gather.2
  483.3 250.5 all-reduce.3
  743.2 303.3 all-reduce.5
  1065.7 255.8 reduce-scatter.3
where the time goes:
time: 1330 us
  waiting for transfers between devices  1260 us (95%)
  matrix products  24.2 us (2%)
  other arithmetic  18 us (1%)
  between operations  15.6 us (1%)
    psum x1, waiting for transfers between devices, on_device(): lax.psum(student_term.astype(jnp.bfloat16), 'tp').astype(jnp.float32)  303 us
    unnamed x6, waiting for transfers between devices  255 us
    psum x1, waiting for transfers between devices, on_device(): lax.psum(teacher_term.astype(jnp.bfloat16), 'tp').astype(jnp.float32)  246 us
    all_gather x1, waiting for transfers between devices, on_device(): lax.all_gather(teacher_weights, 'dp', axis=0, tiled=True)  233 us
    all_gather x1, waiting for transfers between devices, on_device(): lax.all_gather(student_weights, 'dp', axis=0, tiled=True)  226 us
  transfers between devices with their start and end apart: 5, of which 5 were waited for; matrix products, arithmetic and copies ran while one was open for 2% of the time, Pallas kernels for 0%

commit v1 on v0

v1 whole, which is shorter than its diff:
```python
import functools
import math

import jax
import jax.numpy as jnp
from jax import lax
from jax.experimental import pallas as pl
from jax.experimental.pallas import tpu as pltpu
from jax.sharding import PartitionSpec as P

D = 3072
HD = 128
STEPS = 1000
IMAGES = 32
NY, NZ, NX = 4, 8, 4
CH = 4
CW = D // CH
ROWS = D // IMAGES
HALF = ROWS // 2
SEQ = 256
OWN = 16
BF = jnp.bfloat16
F32 = jnp.float32
MESH = pl.DeviceIdType.MESH


def mm(a, b):
    return jnp.dot(a, b, preferred_element_type=F32)


def mm_t(a, b):
    return lax.dot_general(a, b, (((1,), (1,)), ((), ())), preferred_element_type=F32)


def t_mm(a, b):
    return lax.dot_general(a, b, (((0,), (0,)), ((), ())), preferred_element_type=F32)


def kernel(
    time_ref,
    clean_hbm,
    noise_hbm,
    wt_hbm,
    ws_hbm,
    tt_hbm,
    ts_hbm,
    out_v,
    out_g,
    clean,
    noise,
    tables,
    w,
    noisy,
    normed,
    inv,
    trig,
    gates,
    acc,
    proj,
    att,
    att_b,
    attended,
    gated,
    term,
    s_term,
    g_term,
    core_in,
    x_sum,
    x_in,
    z_sum,
    z_in,
    vel,
    gap,
    dnorm,
    grad,
    y_half,
    y_full,
    z_flow,
    load_sem,
    wz_s,
    wz_r,
    wy_s,
    wy_r,
    wh_s,
    wh_r,
    c_s,
    c_r,
    x_s,
    x_r,
    z_s,
    z_r,
    ax_s,
    ax_r,
    ac_s,
    ac_r,
    gh_s,
    gh_r,
    gf_s,
    gf_r,
    gz_s,
    gz_r,
):
    dp, tp = lax.axis_index("dp"), lax.axis_index("tp")
    y, zl = dp // NZ, dp % NZ
    zh, x, c = tp // (2 * NX), (tp // 2) % NX, tp % 2

    def at(yy, zz, hh, xx, cc):
        return (yy * NZ + zz, hh * 2 * NX + xx * 2 + cc)

    def y_to(k):
        return at((y + k + NY) % NY, zl, zh, x, c)

    def z_to(k):
        z = (zh * NZ + zl + k + 2 * NZ) % (2 * NZ)
        return at(y, z % NZ, z // NZ, x, c)

    def x_to(k):
        return at(y, zl, zh, (x + k + NX) % NX, c)

    core_dev = at(y, zl, zh, x, 1 - c)
    far_dev = at(y, zl, 1 - zh, x, c)

    def rcopy(src, dst, send, recv, device):
        return pltpu.make_async_remote_copy(
            src_ref=src, dst_ref=dst, send_sem=send, recv_sem=recv, device_id=device, device_id_type=MESH
        )

    loads = []
    n_load = 0
    for j in range(CH):
        for src, dst in ((clean_hbm, clean), (noise_hbm, noise)):
            loads.append(
                pltpu.make_async_copy(src.at[:, pl.ds(j * CW, CW)], dst.at[j], load_sem.at[n_load])
            )
            n_load += 1
    for m, src in enumerate((tt_hbm, ts_hbm)):
        loads.append(pltpu.make_async_copy(src, tables.at[m], load_sem.at[n_load]))
        n_load += 1
    w_hbm = (wt_hbm, ws_hbm)
    own_w = []
    for m in range(2):
        own_w.append(pltpu.make_async_copy(w_hbm[m], w.at[m, dp], load_sem.at[n_load]))
        n_load += 1
    for copy in own_w + loads:
        copy.start()

    barrier = pltpu.get_barrier_semaphore()
    partners = [z_to(1), z_to(-1), y_to(1), y_to(-1), core_dev, x_to(1), x_to(2), x_to(3), far_dev]
    for device in partners:
        pl.semaphore_signal(barrier, inc=1, device_id=device, device_id_type=MESH)
    pl.semaphore_wait(barrier, len(partners))

    def wblk(m, yy, o):
        return w.at[m, ((yy + NY) % NY) * NZ + o]

    def wz_copy(m, o, way, src=None):
        blk = wblk(m, y, o)
        return rcopy(blk if src is None else src, blk, wz_s.at[m, o, way], wz_r.at[m, o], z_to(1 - 2 * way))

    def wy_copy(m, o, way, src=None):
        blk = wblk(m, y, o)
        return rcopy(blk if src is None else src, blk, wy_s.at[m, o, way], wy_r.at[m, o, way], y_to(1 - 2 * way))

    def wy_arrival(m, o, way):
        blk = wblk(m, y - 1 + 2 * way, o)
        return rcopy(blk, blk, wy_s.at[m, o, way], wy_r.at[m, o, way], y_to(1 - 2 * way))

    def wh_copy(m, o, way):
        blk = wblk(m, y - 1 + 2 * way, o).at[pl.ds(way * HALF, HALF)]
        return rcopy(blk, blk, wh_s.at[m, o, way], wh_r.at[m, o, way], y_to(1 - 2 * way))

    def wh_arrival(m, o, way):
        blk = wblk(m, y + 2, o).at[pl.ds(way * HALF, HALF)]
        return rcopy(blk, blk, wh_s.at[m, o, way], wh_r.at[m, o, way], y_to(1 - 2 * way))

    def w_own(m, with_y):
        @pl.when(zl < NZ - 1)
        def _():
            wz_copy(m, zl, 0, w_hbm[m]).start()

        @pl.when(zl > 0)
        def _():
            wz_copy(m, zl, 1, w_hbm[m]).start()

        if with_y:
            for way in range(2):
                wy_copy(m, zl, way, w_hbm[m]).start()

    def w_zstep(m, s, with_y):
        for way in range(2):
            o = zl - s if way == 0 else zl + s
            there = o >= 0 if way == 0 else o < NZ
            onward = zl < NZ - 1 if way == 0 else zl > 0

            @pl.when(there)
            def _():
                wz_copy(m, o, way).wait_recv()

                @pl.when(onward)
                def _():
                    wz_copy(m, o, way).start()

                if with_y:
                    for side in range(2):
                        wy_copy(m, o, side).start()

    def w_ystart(m):
        for way in range(2):
            wy_copy(m, zl, way, w_hbm[m]).start()

        def body(s, carry):
            for o, there in ((zl - s, zl - s >= 0), (zl + s, zl + s < NZ)):

                @pl.when(there)
                def _():
                    for side in range(2):
                        wy_copy(m, o, side).start()

            return carry

        lax.fori_loop(1, NZ, body, 0)

    def w_ystep(m, s):
        sides = ((zl, zl >= 0),) if s == 0 else ((zl - s, zl - s >= 0), (zl + s, zl + s < NZ))
        for o, there in sides:

            @pl.when(there)
            def _():
                for way in range(2):
                    wy_arrival(m, o, way).wait_recv()
                    wh_copy(m, o, way).start()

    def w_hwait(m):
        def body(o, carry):
            for way in range(2):
                wh_arrival(m, o, way).wait_recv()
            return carry

        lax.fori_loop(0, NZ, body, 0)
        own_w[m].wait()

    def w_drain(m):
        def body(o, carry):
            @pl.when((o <= zl) & (zl < NZ - 1))
            def _():
                wz_copy(m, o, 0).wait_send()

            @pl.when((o >= zl) & (zl > 0))
            def _():
                wz_copy(m, o, 1).wait_send()

            for way in range(2):
                wy_copy(m, o, way).wait_send()
                wh_copy(m, o, way).wait_send()
            return carry

        lax.fori_loop(0, NZ, body, 0)

    def cs_copy(n, buf, j):
        return rcopy(buf.at[j, :, :, 1 - c], core_in.at[n, j], c_s.at[n, j], c_r.at[n, j], core_dev)

    def xs_copy(n, j, k):
        return rcopy(
            x_sum.at[n, j, :, (x + k) % NX], x_in.at[n, j, k - 1], x_s.at[n, j, k - 1], x_r.at[n, j, k - 1], x_to(k)
        )

    def zs_copy(n, j):
        if n == 2:
            return rcopy(z_sum.at[n, j, 1 - zh], z_in.at[n, j, zh], z_s.at[n, j], z_r.at[n, j], far_dev)
        return rcopy(z_sum.at[n, j], z_in.at[n, j], z_s.at[n, j], z_r.at[n, j], far_dev)

    def zs_arrival(n, j):
        if n == 2:
            return rcopy(z_sum.at[n, j, zh], z_in.at[n, j, 1 - zh], z_s.at[n, j], z_r.at[n, j], far_dev)
        return zs_copy(n, j)

    def ax_copy(n, buf, j, k):
        mine = buf.at[j, :, x, c]
        return rcopy(mine, mine, ax_s.at[n, j, k - 1], ax_r.at[n, j, k - 1], x_to(k))

    def ax_arrival(n, buf, j, k):
        blk = buf.at[j, :, (x + NX - k) % NX, c]
        return rcopy(blk, blk, ax_s.at[n, j, k - 1], ax_r.at[n, j, k - 1], x_to(k))

    def ac_copy(n, buf, j, k, cc):
        blk = buf.at[j, :, (x + NX - k) % NX, cc]
        return rcopy(blk, blk, ac_s.at[n, j, k], ac_r.at[n, j, k], core_dev)

    def sum_x_start(n, buf, j):
        cs_copy(n, buf, j).wait_recv()
        for hh in range(2):
            for xx in range(NX):
                total = buf[j, hh, xx, c].astype(F32) + core_in[n, j, hh, xx].astype(F32)
                x_sum[n, j, hh, xx] = total.astype(BF)
        for k in (2, 1, 3):
            xs_copy(n, j, k).start()

    def sum_z_start(n, j):
        for k in range(1, NX):
            xs_copy(n, j, k).wait_recv()
        for hh in range(2):
            total = x_sum[n, j, hh, x].astype(F32)
            for k in range(NX - 1):
                total = total + x_in[n, j, k, hh].astype(F32)
            z_sum[n, j, hh] = total.astype(BF)
        zs_copy(n, j).start()

    def share_start(n, buf, j):
        for k in (2, 1, 3):
            ax_copy(n, buf, j, k).start()
        ac_copy(n, buf, j, 0, c).start()

    def share_forward(n, buf, j):
        for k in (1, 3, 2):
            ax_arrival(n, buf, j, k).wait_recv()
            ac_copy(n, buf, j, k, c).start()

    def share_wait(n, buf, j):
        for k in range(NX):
            ac_copy(n, buf, j, k, 1 - c).wait_recv()

    def sum_drain(n, buf, shared):
        for j in range(CH):
            cs_copy(n, buf, j).wait_send()
            for k in range(1, NX):
                xs_copy(n, j, k).wait_send()
            zs_copy(n, j).wait_send()
            if shared is not None:
                for k in range(1, NX):
                    ax_copy(n, shared, j, k).wait_send()
                for k in range(NX):
                    ac_copy(n, shared, j, k, c).wait_send()

    def project(src, m):
        acc[...] = jnp.zeros_like(acc)

        @pl.loop(0, CH)
        def _(j):
            left = src[j].reshape(SEQ, CW)
            right = w[m, pl.ds(NZ * j, NZ), :, 0 : 3 * HD].reshape(CW, 3 * HD)
            acc[...] += mm(left, right)

        return acc[...].astype(BF)

    scale = HD ** (-0.5)

    def forward(m):
        proj[...] = project(normed, m)
        queries, keys, values = (proj[:, i * HD : (i + 1) * HD] for i in range(3))
        scores = mm_t(queries, keys) * scale
        top = jnp.max(scores, axis=-1, keepdims=True)
        raised = jnp.exp(scores - top)
        probs = raised / jnp.sum(raised, axis=-1, keepdims=True)
        att[...] = probs
        att_b[...] = probs.astype(BF)
        attended[...] = mm(att_b[...], values)
        gated[...] = (attended[...] * (1.0 + gates[pl.ds(m, 1)])).astype(BF)

    def out_columns(m, j):
        return w[m, pl.ds(NZ * j, NZ), :, 3 * HD :].reshape(CW, HD)

    shape6 = (2, NX, 2, OWN, CW)

    w_own(0, True)
    w_own(1, False)

    for copy in loads:
        copy.wait()
    steps = jnp.full((1, CW), time_ref[0].astype(F32))
    step_time = 0.05 + 1.45 * (steps + 0.5) / STEPS
    trig[pl.ds(0, 1)] = jnp.cos(step_time)
    trig[pl.ds(1, 1)] = jnp.sin(step_time)

    @pl.loop(0, 2 * NX * 2)
    def _(r):
        hh, xx, cc = r // (2 * NX), (r // 2) % NX, r % 2
        cosine, sine = trig[pl.ds(0, 1)], trig[pl.ds(1, 1)]
        square = jnp.zeros((OWN, 1), F32)
        for j in range(CH):
            rows = pl.ds(pl.multiple_of(r * OWN, OWN), OWN)
            mixed = cosine * clean[j, rows].astype(F32) + sine * noise[j, rows].astype(F32)
            noisy[j, hh, xx, cc] = mixed
            square = square + jnp.sum(mixed * mixed, axis=-1, keepdims=True)
        factor = lax.rsqrt(square / D + 1e-06)
        inv[hh, xx, cc] = jnp.broadcast_to(factor, (OWN, HD))
        for j in range(CH):
            normed[j, hh, xx, cc] = (noisy[j, hh, xx, cc] * factor).astype(BF)

    half = tables.shape[1] // 2
    position = lax.broadcasted_iota(jnp.int32, (half, HD), 0).astype(F32)
    frequency = 4.0 * jnp.exp(-math.log(100.0) * position / half)
    phases = step_time[:, :HD] * frequency
    cos_p, sin_p = jnp.cos(phases), jnp.sin(phases)
    for m in range(2):
        low, high = tables[m, :half].astype(F32), tables[m, half:].astype(F32)
        gates[pl.ds(m, 1)] = jnp.sum(cos_p * low + sin_p * high, axis=0, keepdims=True)
        if m == 1:
            gates[pl.ds(2, 1)] = jnp.sum(frequency * (cos_p * high - sin_p * low), axis=0, keepdims=True)

    for s in range(1, NZ):
        w_zstep(0, s, True)
        w_ystep(0, s - 1)
        w_zstep(1, s, False)
    w_ystep(0, NZ - 1)
    w_ystart(1)
    w_hwait(0)

    forward(0)
    for j in range(CH):
        term[j] = mm_t(gated[...], out_columns(0, j)).astype(BF).reshape(shape6)
        cs_copy(0, term, j).start()

    def velocity_rows(j):
        zs_arrival(0, j).wait_recv()
        for hh in range(2):
            total = z_sum[0, j, hh].astype(F32) + z_in[0, j, hh].astype(F32)
            vel[j, hh, x, c] = (noisy[j, hh, x, c] + total).astype(BF)
        share_start(0, vel, j)

    for j in range(CH):
        sum_x_start(0, term, j)
    w_ystep(1, 0)
    for j in range(CH):
        sum_z_start(0, j)
        w_ystep(1, j + 1)
    for j in range(CH):
        velocity_rows(j)
        if j + CH + 1 < NZ:
            w_ystep(1, j + CH + 1)
    for j in range(CH):
        share_forward(0, vel, j)
    w_hwait(1)

    forward(1)
    for j in range(CH):
        s_term[j] = mm_t(gated[...], out_columns(1, j)).astype(BF).reshape(shape6)
    for j in range(CH):
        share_wait(0, vel, j)

    @pl.loop(0, 2 * NX * 2)
    def _(r):
        hh, xx, cc = r // (2 * NX), (r // 2) % NX, r % 2
        factor = inv[hh, xx, cc][:, :1]
        inner = jnp.zeros((OWN, 1), F32)
        for j in range(CH):
            product = noisy[j, hh, xx, cc] * factor * vel[j, hh, xx, cc].astype(F32)
            inner = inner + jnp.sum(product, axis=-1, keepdims=True)
        inner = inner / D
        for j in range(CH):
            whole = noisy[j, hh, xx, cc] * factor
            dnorm[j, hh, xx, cc] = (factor * (vel[j, hh, xx, cc].astype(F32) - whole * inner)).astype(BF)

    d_proj = project(dnorm, 1)
    d_queries, d_keys, d_values = (d_proj[:, i * HD : (i + 1) * HD] for i in range(3))
    d_scores = (mm_t(d_queries, proj[:, HD : 2 * HD]) + mm_t(proj[:, :HD], d_keys)) * scale
    probs = att[...]
    d_probs = probs * (d_scores - jnp.sum(probs * d_scores, axis=-1, keepdims=True))
    d_attended = mm(d_probs.astype(BF), proj[:, 2 * HD :]) + mm(att_b[...], d_values)
    d_gated = (d_attended * (1.0 + gates[1:2]) + attended[...] * gates[2:3]).astype(BF)
    for j in range(CH):
        d_term = mm_t(d_gated, out_columns(1, j)).astype(BF).astype(F32)
        cosine, sine = trig[0:1], trig[1:2]
        both = cosine * cosine * s_term[j].reshape(SEQ, CW).astype(F32) + cosine * sine * d_term
        g_term[j] = both.astype(BF).reshape(shape6)
        cs_copy(1, g_term, j).start()

    def gap_rows(j):
        zs_arrival(1, j).wait_recv()
        cosine, sine = trig[0:1], trig[1:2]
        for hh in range(2):
            total = z_sum[1, j, hh].astype(F32) + z_in[1, j, hh].astype(F32)
            clear = -(cosine * cosine + cosine * sine) * noisy[j, hh, x, c]
            moved = (cosine * cosine - cosine * sine) * vel[j, hh, x, c].astype(F32)
            gap[j, hh, x, c] = (clear + moved - total).astype(BF)
        share_start(1, gap, j)

    for j in range(CH):
        sum_x_start(1, g_term, j)
    for j in range(CH):
        cs_copy(2, s_term, j).start()
    for j in range(CH):
        sum_z_start(1, j)
    for j in range(CH):
        sum_x_start(2, s_term, j)
    for j in range(CH):
        gap_rows(j)
    for j in range(CH):
        share_forward(1, gap, j)
    for j in range(CH):
        sum_z_start(2, j)
    for j in range(CH):
        share_wait(1, gap, j)

    square = jnp.zeros((1, 1), F32)
    back = jnp.zeros((SEQ, HD), F32)
    for j in range(CH):
        whole = gap[j].reshape(SEQ, CW)
        wide = whole.astype(F32)
        rows = jnp.sum(wide * wide, axis=0, keepdims=True)
        square = square + jnp.sum(rows, axis=1, keepdims=True)
        back = back + mm(whole, out_columns(1, j))
    cot = -math.sqrt(D / IMAGES) / (jnp.sqrt(square) + 0.1)
    d_att_b = (back * cot * (1.0 + gates[1:2])).astype(BF)
    queries, keys, values = (proj[:, i * HD : (i + 1) * HD] for i in range(3))
    grad_values = t_mm(att_b[...], d_att_b)
    d_back = mm_t(d_att_b, values)
    probs = att[...]
    d_scores_b = (probs * (d_back - jnp.sum(probs * d_back, axis=-1, keepdims=True)) * scale).astype(BF)
    grad_queries = mm(d_scores_b, keys)
    grad_keys = t_mm(d_scores_b, queries)
    d_proj_b = jnp.concatenate([grad_queries, grad_keys, grad_values], axis=1).astype(BF)

    def gh_copy(d, way):
        part = pl.ds(way * HALF, HALF)
        return rcopy(
            grad.at[(y + 2) % NY, d, part], y_half.at[way, d], gh_s.at[way, d], gh_r.at[way, d], y_to(1 - 2 * way)
        )

    def gf_copy(d, way):
        return rcopy(
            grad.at[(y + 1 - 2 * way + NY) % NY, d],
            y_full.at[way, d],
            gf_s.at[way, d],
            gf_r.at[way, d],
            y_to(1 - 2 * way),
        )

    def gz_copy(d, way):
        return rcopy(grad.at[y, d], z_flow.at[way, d], gz_s.at[d], gz_r.at[way, d], z_to(1 - 2 * way))

    for k in (2, 1, 3, 0):
        yy = (y + k) % NY
        left = t_mm(normed[yy].reshape(SEQ, CW), d_proj_b)
        grad[yy, :, :, 0 : 3 * HD] = left.astype(BF).reshape(NZ, ROWS, 3 * HD)
        right = t_mm(gap[yy].reshape(SEQ, CW), gated[...]) * cot
        grad[yy, :, :, 3 * HD :] = right.astype(BF).reshape(NZ, ROWS, HD)
        if k == 2:

            @pl.loop(0, NZ)
            def _(i):
                d = jnp.where(i % 2 == 0, NZ - 1 - i // 2, i // 2)
                for way in range(2):
                    gh_copy(d, way).start()

    def order(i):
        return jnp.where(i % 2 == 0, NZ - 1 - i // 2, i // 2)

    def reduced(d):
        for way in range(2):
            gf_copy(d, way).wait_recv()
        return grad[y, d].astype(F32) + y_full[0, d].astype(F32) + y_full[1, d].astype(F32)

    @pl.loop(0, 13)
    def _(t):
        @pl.when(t < NZ)
        def _():
            d = order(t)
            for way in range(2):
                gh_copy(d, way).wait_recv()
                yy = (y + 1 - 2 * way + NY) % NY
                part = pl.ds(way * HALF, HALF)
                total = grad[yy, d, part].astype(F32) + y_half[way, d].astype(F32)
                grad[yy, d, part] = total.astype(BF)
                gf_copy(d, way).start()

        for way in range(2):
            hops = zl if way == 0 else NZ - 1 - zl
            i = t - 1 - hops
            ok = (i >= 0) & (i < NZ)
            d = order(jnp.clip(i, 0, NZ - 1))

            @pl.when(ok & ((zl < d) if way == 0 else (zl > d)))
            def _():
                total = reduced(d)

                @pl.when(hops > 0)
                def _():
                    gz_copy(d, way).wait_recv()
                    grad[y, d] = (total + z_flow[way, d].astype(F32)).astype(BF)

                @pl.when(hops == 0)
                def _():
                    grad[y, d] = total.astype(BF)

                gz_copy(d, way).start()

        @pl.when(t == 12)
        def _():
            total = reduced(zl)

            @pl.when(zl > 0)
            def _():
                gz_copy(zl, 0).wait_recv()

            @pl.when(zl < NZ - 1)
            def _():
                gz_copy(zl, 1).wait_recv()

            @pl.when(zl == 0)
            def _():
                out_g[...] = (total + z_flow[1, zl].astype(F32)).astype(BF)

            @pl.when(zl == NZ - 1)
            def _():
                out_g[...] = (total + z_flow[0, zl].astype(F32)).astype(BF)

            @pl.when((zl > 0) & (zl < NZ - 1))
            def _():
                out_g[...] = (total + z_flow[0, zl].astype(F32) + z_flow[1, zl].astype(F32)).astype(BF)

    for j in range(CH):
        zs_arrival(2, j).wait_recv()
        total = z_sum[2, j, zh].astype(F32) + z_in[2, j, 1 - zh].astype(F32)
        out_v[:, j * CW : (j + 1) * CW] = (noisy[j, zh, x, c] + total).astype(BF)

    w_drain(0)
    w_drain(1)
    sum_drain(0, term, vel)
    sum_drain(1, g_term, gap)
    sum_drain(2, s_term, None)

    @pl.loop(0, NZ)
    def _(d):
        for way in range(2):
            gh_copy(d, way).wait_send()
            gf_copy(d, way).wait_send()

        @pl.when(d != zl)
        def _():
            gz_copy(d, 0).wait_send()


def on_device(clean, noise, time_index, teacher_w, student_w, teacher_t, student_t):
    blocks = (CH, 2, NX, 2, OWN, CW)
    dma = pltpu.SemaphoreType.DMA
    scratch = [
        pltpu.VMEM((CH, SEQ, CW), BF),
        pltpu.VMEM((CH, SEQ, CW), BF),
        pltpu.VMEM((2,) + teacher_t.shape, BF),
        pltpu.VMEM((2, IMAGES, ROWS, 4 * HD), BF),
        pltpu.VMEM(blocks, F32),
        pltpu.VMEM(blocks, BF),
        pltpu.VMEM((2, NX, 2, OWN, HD), F32),
        pltpu.VMEM((8, CW), F32),
        pltpu.VMEM((8, HD), F32),
        pltpu.VMEM((SEQ, 3 * HD), F32),
        pltpu.VMEM((SEQ, 3 * HD), BF),
        pltpu.VMEM((SEQ, SEQ), F32),
        pltpu.VMEM((SEQ, SEQ), BF),
        pltpu.VMEM((SEQ, HD), F32),
        pltpu.VMEM((SEQ, HD), BF),
        pltpu.VMEM(blocks, BF),
        pltpu.VMEM(blocks, BF),
        pltpu.VMEM(blocks, BF),
        pltpu.VMEM((3, CH, 2, NX, OWN, CW), BF),
        pltpu.VMEM((3, CH, 2, NX, OWN, CW), BF),
        pltpu.VMEM((3, CH, NX - 1, 2, OWN, CW), BF),
        pltpu.VMEM((3, CH, 2, OWN, CW), BF),
        pltpu.VMEM((3, CH, 2, OWN, CW), BF),
        pltpu.VMEM(blocks, BF),
        pltpu.VMEM(blocks, BF),
        pltpu.VMEM(blocks, BF),
        pltpu.VMEM((NY, NZ, ROWS, 4 * HD), BF),
        pltpu.VMEM((2, NZ, HALF, 4 * HD), BF),
        pltpu.VMEM((2, NZ, ROWS, 4 * HD), BF),
        pltpu.VMEM((2, NZ, ROWS, 4 * HD), BF),
        dma((2 * CH + 4,)),
        dma((2, NZ, 2)),
        dma((2, NZ)),
        dma((2, NZ, 2)),
        dma((2, NZ, 2)),
        dma((2, NZ, 2)),
        dma((2, NZ, 2)),
        dma((3, CH)),
        dma((3, CH)),
        dma((3, CH, NX - 1)),
        dma((3, CH, NX - 1)),
        dma((3, CH)),
        dma((3, CH)),
        dma((2, CH, NX - 1)),
        dma((2, CH, NX - 1)),
        dma((2, CH, NX)),
        dma((2, CH, NX)),
        dma((2, NZ)),
        dma((2, NZ)),
        dma((2, NZ)),
        dma((2, NZ)),
        dma((NZ,)),
        dma((2, NZ)),
    ]
    out_v, out_g = pl.pallas_call(
        kernel,
        name="distill_step",
        out_shape=(jax.ShapeDtypeStruct((OWN, D), BF), jax.ShapeDtypeStruct((ROWS, 4 * HD), BF)),
        in_specs=[pl.BlockSpec(memory_space=pltpu.SMEM)] + [pl.BlockSpec(memory_space=pl.ANY)] * 6,
        out_specs=(pl.BlockSpec(memory_space=pltpu.VMEM), pl.BlockSpec(memory_space=pltpu.VMEM)),
        scratch_shapes=scratch,
        compiler_params=pltpu.CompilerParams(
            collective_id=0, has_side_effects=True, vmem_limit_bytes=60 * 1024 * 1024
        ),
        cost_estimate=pl.CostEstimate(flops=4_000_000_000, bytes_accessed=4_000_000, transcendentals=200_000),
    )(time_index, clean[0], noise[0], teacher_w, student_w, teacher_t, student_t)
    return (out_v[None], out_g)


def solution(mesh):
    placed = (
        P("dp", None, None),
        P("dp", None, None),
        P("dp"),
        P("dp", "tp"),
        P("dp", "tp"),
        P(None, "tp"),
        P(None, "tp"),
    )
    return jax.shard_map(
        on_device,
        mesh=mesh,
        in_specs=placed,
        out_specs=(P("dp", "tp", None), P("dp", "tp")),
        check_vma=False,
    )
```

time: 1330 us -> 195 us (0.15)
  the two profiles are of different devices: /device:TPU:2 before, /device:TPU:66 now
where the time goes in v1:
time: 195 us; the launch traced here: 194 us
  Pallas kernels  190 us (97%)
  local copies, waits for them, and re-layouts  3.08 us (2%)
    pallas_call x1, Pallas kernels, on_device(): pl.pallas_call(kernel, name='distill_step', out_shape=(jax.ShapeDtypeStru...  190 us

profile of v1, /device:TPU:66, one launch (start us, length us, event | category | flops | bytes accessed | tf_op | source)
XLA Modules:
  0.0 194.5 jit_solution(9932048920996767124)
XLA Ops:
  1.3 190.1 %distill_step.1 = (bf16[16,3072]{1,0:T(8,128)(2,1)}, bf16[96,512]{1,0:T(8,128)(2,1)}) custom-call(s32[1]{0:T(128)S(6)} %copy.11.time_ref, bf16[256,3072]{1,0:T(8,128)(2,1)} %bitcast.4, bf16[256,3072]{1,0:T(8,128)(2,1)} %bitcast.5, bf16[96,512]{1,0:T(8,128)(2,1)} %wt_hbm.1, bf16[96,512]{1,0:T(8,128)(2,1)} %ws_hbm.1, bf16[256,128]{1,0:T(8,128)(2,1)} %tt_hbm.1, ...), custom_call_target="tpu_custom_call" | custom-call | flops 4000000000 | bytes 4000000 | tf_op jit(solution)/shard_map/distill_step/pallas_call | solution.py:691
  191.4 1.5 copy.12
  192.9 1.5 copy.13

commit v2 on v1

--- a/solution.py
+++ b/solution.py
@@ -13,6 +13,7 @@
 STEPS = 1000
 IMAGES = 32
 NY, NZ, NX = 4, 8, 4
+NG = NZ // 2
 CH = 4
 CW = D // CH
 ROWS = D // IMAGES
@@ -71,7 +72,6 @@
     z_in,
     vel,
     gap,
-    dnorm,
     grad,
     y_half,
     y_full,
@@ -111,8 +111,7 @@
         return at((y + k + NY) % NY, zl, zh, x, c)
 
     def z_to(k):
-        z = (zh * NZ + zl + k + 2 * NZ) % (2 * NZ)
-        return at(y, z % NZ, z // NZ, x, c)
+        return at(y, (zl + k + NZ) % NZ, zh, x, c)
 
     def x_to(k):
         return at(y, zl, zh, (x + k + NX) % NX, c)
@@ -145,94 +144,102 @@
         copy.start()
 
     barrier = pltpu.get_barrier_semaphore()
-    partners = [z_to(1), z_to(-1), y_to(1), y_to(-1), core_dev, x_to(1), x_to(2), x_to(3), far_dev]
+    partners = [far_dev, z_to(NG), z_to(1), z_to(-1), x_to(2), y_to(1), y_to(-1), x_to(1), x_to(3), core_dev]
     for device in partners:
         pl.semaphore_signal(barrier, inc=1, device_id=device, device_id_type=MESH)
     pl.semaphore_wait(barrier, len(partners))
 
-    def wblk(m, yy, o):
-        return w.at[m, ((yy + NY) % NY) * NZ + o]
-
-    def wz_copy(m, o, way, src=None):
-        blk = wblk(m, y, o)
-        return rcopy(blk if src is None else src, blk, wz_s.at[m, o, way], wz_r.at[m, o], z_to(1 - 2 * way))
-
-    def wy_copy(m, o, way, src=None):
-        blk = wblk(m, y, o)
-        return rcopy(blk if src is None else src, blk, wy_s.at[m, o, way], wy_r.at[m, o, way], y_to(1 - 2 * way))
-
-    def wy_arrival(m, o, way):
-        blk = wblk(m, y - 1 + 2 * way, o)
-        return rcopy(blk, blk, wy_s.at[m, o, way], wy_r.at[m, o, way], y_to(1 - 2 * way))
+    inner_r, inner_l = zl < NZ - 1, zl > 0
+    events = [
+        (zl, zl >= 0, 3, inner_r, inner_l),
+        (zl - 1, zl >= 1, 0, inner_r, None),
+        (zl + 1, zl + 1 < NZ, 1, None, inner_l),
+        ((zl + NG) % NZ, zl >= 0, 2, inner_r, inner_l),
+        (zl - 2, zl >= 2, 0, inner_r & (zl - 2 >= NG), None),
+        (zl + 2, zl + 2 < NZ, 1, None, inner_l & (zl + 2 < NG)),
+        ((zl + 3) % NZ, inner_l, 0, inner_r & (zl >= 5), None),
+        ((zl + 5) % NZ, inner_r, 1, None, inner_l & (zl <= 2)),
+        (zl - 3, zl - 3 >= NG, 0, None, None),
+        (zl + 3, zl + 3 < NG, 1, None, None),
+        (zl - 6, zl >= 6, 0, inner_r, None),
+        (zl + 6, zl + 6 < NZ, 1, None, inner_l),
+        (zl - 7, zl >= 7, 0, None, None),
+        (zl + 7, zl + 7 < NZ, 1, None, None),
+    ]
+
+    def wblk(m, yy, o, p):
+        return w.at[m, ((yy + NY) % NY) * NZ + o, pl.ds(p * HALF, HALF)]
+
+    def wz_copy(m, o, way, own=False):
+        blk = w.at[m, y * NZ + o]
+        src = w_hbm[m] if own else blk
+        device = z_to((1, -1, NG)[way])
+        return rcopy(src, blk, wz_s.at[m, o, way], wz_r.at[m, o], device)
+
+    def when(there):
+        return (lambda f: None) if there is None else pl.when(there)
+
+    def wy_copy(m, o, way, p, own=False):
+        blk = wblk(m, y, o, p)
+        src = w_hbm[m].at[pl.ds(p * HALF, HALF)] if own else blk
+        return rcopy(src, blk, wy_s.at[m, o, way, p], wy_r.at[m, o, way, p], y_to(1 - 2 * way))
+
+    def wy_arrival(m, o, way, p):
+        blk = wblk(m, y - 1 + 2 * way, o, p)
+        return rcopy(blk, blk, wy_s.at[m, o, way, p], wy_r.at[m, o, way, p], y_to(1 - 2 * way))
 
     def wh_copy(m, o, way):
-        blk = wblk(m, y - 1 + 2 * way, o).at[pl.ds(way * HALF, HALF)]
+        blk = wblk(m, y - 1 + 2 * way, o, way)
         return rcopy(blk, blk, wh_s.at[m, o, way], wh_r.at[m, o, way], y_to(1 - 2 * way))
 
     def wh_arrival(m, o, way):
-        blk = wblk(m, y + 2, o).at[pl.ds(way * HALF, HALF)]
+        blk = wblk(m, y + 2, o, way)
         return rcopy(blk, blk, wh_s.at[m, o, way], wh_r.at[m, o, way], y_to(1 - 2 * way))
 
-    def w_own(m, with_y):
-        @pl.when(zl < NZ - 1)
+    def wy_start(m, o, own=False):
+        for p in range(2):
+            for way in range(2):
+                wy_copy(m, o, way, (p + way) % 2, own).start()
+
+    def w_zstep(m, e, with_y=True):
+        o, there, side, right, left = events[e]
+
+        @pl.when(there)
         def _():
-            wz_copy(m, zl, 0, w_hbm[m]).start()
-
-        @pl.when(zl > 0)
+            if e:
+                wz_copy(m, o, 0).wait_recv()
+            else:
+                wz_copy(m, o, 2, True).start()
+
+            @when(right)
+            def _():
+                wz_copy(m, o, 0, e == 0).start()
+
+            @when(left)
+            def _():
+                wz_copy(m, o, 1, e == 0).start()
+
+            if with_y:
+                wy_start(m, o, e == 0)
+
+    def wy_later(m, e):
+        @pl.when(events[e][1])
         def _():
-            wz_copy(m, zl, 1, w_hbm[m]).start()
-
-        if with_y:
+            wy_start(m, events[e][0], e == 0)
+
+    def w_ystep(m, e):
+        o, there = events[e][:2]
+
+        @pl.when(there)
+        def _():
             for way in range(2):
-                wy_copy(m, zl, way, w_hbm[m]).start()
-
-    def w_zstep(m, s, with_y):
-        for way in range(2):
-            o = zl - s if way == 0 else zl + s
-            there = o >= 0 if way == 0 else o < NZ
-            onward = zl < NZ - 1 if way == 0 else zl > 0
-
-            @pl.when(there)
-            def _():
-                wz_copy(m, o, way).wait_recv()
-
-                @pl.when(onward)
-                def _():
-                    wz_copy(m, o, way).start()
-
-                if with_y:
-                    for side in range(2):
-                        wy_copy(m, o, side).start()
-
-    def w_ystart(m):
-        for way in range(2):
-            wy_copy(m, zl, way, w_hbm[m]).start()
-
-        def body(s, carry):
-            for o, there in ((zl - s, zl - s >= 0), (zl + s, zl + s < NZ)):
-
-                @pl.when(there)
-                def _():
-                    for side in range(2):
-                        wy_copy(m, o, side).start()
-
-            return carry
-
-        lax.fori_loop(1, NZ, body, 0)
-
-    def w_ystep(m, s):
-        sides = ((zl, zl >= 0),) if s == 0 else ((zl - s, zl - s >= 0), (zl + s, zl + s < NZ))
-        for o, there in sides:
-
-            @pl.when(there)
-            def _():
-                for way in range(2):
-                    wy_arrival(m, o, way).wait_recv()
-                    wh_copy(m, o, way).start()
+                wy_arrival(m, o, way, way).wait_recv()
+                wh_copy(m, o, way).start()
 
     def w_hwait(m):
         def body(o, carry):
             for way in range(2):
+                wy_arrival(m, o, way, 1 - way).wait_recv()
                 wh_arrival(m, o, way).wait_recv()
             return carry
 
@@ -240,17 +247,19 @@
         own_w[m].wait()
 
     def w_drain(m):
+        wz_copy(m, zl, 2).wait_send()
+        for o, there, side, right, left in events:
+            for way, onward in ((0, right), (1, left)):
+                if onward is not None:
+
+                    @pl.when(there & onward)
+                    def _():
+                        wz_copy(m, o, way).wait_send()
+
         def body(o, carry):
-            @pl.when((o <= zl) & (zl < NZ - 1))
-            def _():
-                wz_copy(m, o, 0).wait_send()
-
-            @pl.when((o >= zl) & (zl > 0))
-            def _():
-                wz_copy(m, o, 1).wait_send()
-
             for way in range(2):
-                wy_copy(m, o, way).wait_send()
+                for p in range(2):
+                    wy_copy(m, o, way, p).wait_send()
                 wh_copy(m, o, way).wait_send()
             return carry
 
@@ -344,8 +353,7 @@
 
     scale = HD ** (-0.5)
 
-    def forward(m):
-        proj[...] = project(normed, m)
+    def attend(m):
         queries, keys, values = (proj[:, i * HD : (i + 1) * HD] for i in range(3))
         scores = mm_t(queries, keys) * scale
         top = jnp.max(scores, axis=-1, keepdims=True)
@@ -361,18 +369,36 @@
 
     shape6 = (2, NX, 2, OWN, CW)
 
-    w_own(0, True)
-    w_own(1, False)
-
-    for copy in loads:
+    w_zstep(0, 0)
+
+    for e in range(1, 4):
+        w_zstep(0, e)
+    for copy in loads[2 * CH :]:
         copy.wait()
     steps = jnp.full((1, CW), time_ref[0].astype(F32))
     step_time = 0.05 + 1.45 * (steps + 0.5) / STEPS
     trig[pl.ds(0, 1)] = jnp.cos(step_time)
     trig[pl.ds(1, 1)] = jnp.sin(step_time)
 
-    @pl.loop(0, 2 * NX * 2)
-    def _(r):
+    half = tables.shape[1] // 2
+    position = lax.broadcasted_iota(jnp.int32, (half, HD), 0).astype(F32)
+    frequency = 4.0 * jnp.exp(-math.log(100.0) * position / half)
+    phases = step_time[:, :HD] * frequency
+    cos_p, sin_p = jnp.cos(phases), jnp.sin(phases)
+    for m in range(2):
+        low, high = tables[m, :half].astype(F32), tables[m, half:].astype(F32)
+        gates[pl.ds(m, 1)] = jnp.sum(cos_p * low + sin_p * high, axis=0, keepdims=True)
+        if m == 1:
+            gates[pl.ds(2, 1)] = jnp.sum(frequency * (cos_p * high - sin_p * low), axis=0, keepdims=True)
+
+    for e in range(4, 8):
+        w_zstep(0, e)
+    for e in (0, 1, 2):
+        w_ystep(0, e)
+    for copy in loads[: 2 * CH]:
+        copy.wait()
+
+    def mix(r):
         hh, xx, cc = r // (2 * NX), (r // 2) % NX, r % 2
         cosine, sine = trig[pl.ds(0, 1)], trig[pl.ds(1, 1)]
         square = jnp.zeros((OWN, 1), F32)
@@ -386,29 +412,33 @@
         for j in range(CH):
             normed[j, hh, xx, cc] = (noisy[j, hh, xx, cc] * factor).astype(BF)
 
-    half = tables.shape[1] // 2
-    position = lax.broadcasted_iota(jnp.int32, (half, HD), 0).astype(F32)
-    frequency = 4.0 * jnp.exp(-math.log(100.0) * position / half)
-    phases = step_time[:, :HD] * frequency
-    cos_p, sin_p = jnp.cos(phases), jnp.sin(phases)
-    for m in range(2):
-        low, high = tables[m, :half].astype(F32), tables[m, half:].astype(F32)
-        gates[pl.ds(m, 1)] = jnp.sum(cos_p * low + sin_p * high, axis=0, keepdims=True)
-        if m == 1:
-            gates[pl.ds(2, 1)] = jnp.sum(frequency * (cos_p * high - sin_p * low), axis=0, keepdims=True)
-
-    for s in range(1, NZ):
-        w_zstep(0, s, True)
-        w_ystep(0, s - 1)
-        w_zstep(1, s, False)
-    w_ystep(0, NZ - 1)
-    w_ystart(1)
+    def mix_rows(first, end):
+        pl.loop(first, end)(mix)
+
+    mix_rows(0, 6)
+    for e in range(8, 12):
+        w_zstep(0, e)
+    for e in (3, 4, 5):
+        w_ystep(0, e)
+    mix_rows(6, 11)
+    for e in (12, 13):
+        w_zstep(0, e)
+    w_zstep(1, 0, False)
+    mix_rows(11, 16)
+    for e in (6, 7, 8, 9, 10, 11, 12, 13):
+        w_ystep(0, e)
     w_hwait(0)
-
-    forward(0)
+    wy_later(1, 0)
+    for e in (1, 2, 3):
+        w_zstep(1, e)
+
+    proj[...] = project(normed, 0)
+    attend(0)
     for j in range(CH):
         term[j] = mm_t(gated[...], out_columns(0, j)).astype(BF).reshape(shape6)
         cs_copy(0, term, j).start()
+    for e in (4, 5, 6, 7):
+        w_zstep(1, e)
 
     def velocity_rows(j):
         zs_arrival(0, j).wait_recv()
@@ -419,38 +449,43 @@
 
     for j in range(CH):
         sum_x_start(0, term, j)
-    w_ystep(1, 0)
+    for e in (8, 9, 10, 11):
+        w_zstep(1, e)
     for j in range(CH):
         sum_z_start(0, j)
-        w_ystep(1, j + 1)
-    for j in range(CH):
-        velocity_rows(j)
-        if j + CH + 1 < NZ:
-            w_ystep(1, j + CH + 1)
-    for j in range(CH):
-        share_forward(0, vel, j)
+    for e in (12, 13):
+        w_zstep(1, e)
+    for e in (0, 1, 2, 3, 4, 5, 6, 7):
+        w_ystep(1, e)
+    velocity_rows(0)
+    for e in (8, 9, 10, 11):
+        w_ystep(1, e)
+    velocity_rows(1)
+    share_forward(0, vel, 0)
+    for e in (12, 13):
+        w_ystep(1, e)
+    velocity_rows(2)
+    share_forward(0, vel, 1)
+    velocity_rows(3)
+    share_forward(0, vel, 2)
     w_hwait(1)
-
-    forward(1)
+    proj[...] = project(normed, 1)
+
+    attend(1)
+    share_forward(0, vel, 3)
     for j in range(CH):
         s_term[j] = mm_t(gated[...], out_columns(1, j)).astype(BF).reshape(shape6)
+
+    moved = jnp.zeros((SEQ, 3 * HD), F32)
+    inner = jnp.zeros((SEQ, 1), F32)
     for j in range(CH):
         share_wait(0, vel, j)
-
-    @pl.loop(0, 2 * NX * 2)
-    def _(r):
-        hh, xx, cc = r // (2 * NX), (r // 2) % NX, r % 2
-        factor = inv[hh, xx, cc][:, :1]
-        inner = jnp.zeros((OWN, 1), F32)
-        for j in range(CH):
-            product = noisy[j, hh, xx, cc] * factor * vel[j, hh, xx, cc].astype(F32)
-            inner = inner + jnp.sum(product, axis=-1, keepdims=True)
-        inner = inner / D
-        for j in range(CH):
-            whole = noisy[j, hh, xx, cc] * factor
-            dnorm[j, hh, xx, cc] = (factor * (vel[j, hh, xx, cc].astype(F32) - whole * inner)).astype(BF)
-
-    d_proj = project(dnorm, 1)
+        arrived = vel[j].reshape(SEQ, CW)
+        product = noisy[j].reshape(SEQ, CW) * arrived.astype(F32)
+        inner = inner + jnp.sum(product, axis=-1, keepdims=True)
+        moved = moved + mm(arrived, w[1, NZ * j : NZ * (j + 1), :, 0 : 3 * HD].reshape(CW, 3 * HD))
+    factor = inv[...].reshape(SEQ, HD)[:, :1]
+    d_proj = (factor * (moved - factor * inner / D * acc[...])).astype(BF)
     d_queries, d_keys, d_values = (d_proj[:, i * HD : (i + 1) * HD] for i in range(3))
     d_scores = (mm_t(d_queries, proj[:, HD : 2 * HD]) + mm_t(proj[:, :HD], d_keys)) * scale
     probs = att[...]
@@ -482,18 +517,23 @@
         sum_z_start(1, j)
     for j in range(CH):
         sum_x_start(2, s_term, j)
-    for j in range(CH):
-        gap_rows(j)
-    for j in range(CH):
-        share_forward(1, gap, j)
-    for j in range(CH):
-        sum_z_start(2, j)
-    for j in range(CH):
-        share_wait(1, gap, j)
+    gap_rows(0)
+    gap_rows(1)
+    share_forward(1, gap, 0)
+    sum_z_start(2, 0)
+    sum_z_start(2, 1)
+    gap_rows(2)
+    share_forward(1, gap, 1)
+    sum_z_start(2, 2)
+    sum_z_start(2, 3)
+    gap_rows(3)
+    share_forward(1, gap, 2)
+    share_forward(1, gap, 3)
 
     square = jnp.zeros((1, 1), F32)
     back = jnp.zeros((SEQ, HD), F32)
     for j in range(CH):
+        share_wait(1, gap, j)
         whole = gap[j].reshape(SEQ, CW)
         wide = whole.astype(F32)
         rows = jnp.sum(wide * wide, axis=0, keepdims=True)
@@ -526,7 +566,11 @@
         )
 
     def gz_copy(d, way):
-        return rcopy(grad.at[y, d], z_flow.at[way, d], gz_s.at[d], gz_r.at[way, d], z_to(1 - 2 * way))
+        dst = z_flow.at[2, 0] if way == 2 else z_flow.at[way, d]
+        recv = gz_r.at[2, 0] if way == 2 else gz_r.at[way, d]
+        return rcopy(grad.at[y, d], dst, gz_s.at[d], recv, z_to((-1, 1, NG)[way]))
+
+    late_first = (12, 13, 10, 11, 6, 7, 8, 9, 3, 4, 5, 1, 2, 0)
 
     for k in (2, 1, 3, 0):
         yy = (y + k) % NY
@@ -536,77 +580,48 @@
         grad[yy, :, :, 3 * HD :] = right.astype(BF).reshape(NZ, ROWS, HD)
         if k == 2:
 
-            @pl.loop(0, NZ)
-            def _(i):
-                d = jnp.where(i % 2 == 0, NZ - 1 - i // 2, i // 2)
-                for way in range(2):
-                    gh_copy(d, way).start()
-
-    def order(i):
-        return jnp.where(i % 2 == 0, NZ - 1 - i // 2, i // 2)
-
-    def reduced(d):
+            for e in late_first:
+
+                @pl.when(events[e][1])
+                def _():
+                    for way in range(2):
+                        gh_copy(events[e][0], way).start()
+
+    def y_second(d):
         for way in range(2):
-            gf_copy(d, way).wait_recv()
-        return grad[y, d].astype(F32) + y_full[0, d].astype(F32) + y_full[1, d].astype(F32)
-
-    @pl.loop(0, 13)
-    def _(t):
-        @pl.when(t < NZ)
+            gh_copy(d, way).wait_recv()
+            yy = (y + 1 - 2 * way + NY) % NY
+            part = pl.ds(way * HALF, HALF)
+            total = grad[yy, d, part].astype(F32) + y_half[way, d].astype(F32)
+            grad[yy, d, part] = total.astype(BF)
+            gf_copy(d, way).start()
+
+    for e in late_first:
+
+        @pl.when(events[e][1])
         def _():
-            d = order(t)
+            y_second(events[e][0])
+
+    for e in late_first:
+        d, there, side, right, left = events[e]
+
+        @pl.when(there)
+        def _():
             for way in range(2):
-                gh_copy(d, way).wait_recv()
-                yy = (y + 1 - 2 * way + NY) % NY
-                part = pl.ds(way * HALF, HALF)
-                total = grad[yy, d, part].astype(F32) + y_half[way, d].astype(F32)
-                grad[yy, d, part] = total.astype(BF)
-                gf_copy(d, way).start()
-
-        for way in range(2):
-            hops = zl if way == 0 else NZ - 1 - zl
-            i = t - 1 - hops
-            ok = (i >= 0) & (i < NZ)
-            d = order(jnp.clip(i, 0, NZ - 1))
-
-            @pl.when(ok & ((zl < d) if way == 0 else (zl > d)))
-            def _():
-                total = reduced(d)
-
-                @pl.when(hops > 0)
+                gf_copy(d, way).wait_recv()
+            grad[y, d] = (grad[y, d].astype(F32) + y_full[0, d].astype(F32) + y_full[1, d].astype(F32)).astype(BF)
+            for way, child in ((0, right), (1, left)):
+
+                @when(child)
                 def _():
                     gz_copy(d, way).wait_recv()
-                    grad[y, d] = (total + z_flow[way, d].astype(F32)).astype(BF)
-
-                @pl.when(hops == 0)
-                def _():
-                    grad[y, d] = total.astype(BF)
-
-                gz_copy(d, way).start()
-
-        @pl.when(t == 12)
-        def _():
-            total = reduced(zl)
-
-            @pl.when(zl > 0)
-            def _():
-                gz_copy(zl, 0).wait_recv()
-
-            @pl.when(zl < NZ - 1)
-            def _():
-                gz_copy(zl, 1).wait_recv()
-
-            @pl.when(zl == 0)
-            def _():
-                out_g[...] = (total + z_flow[1, zl].astype(F32)).astype(BF)
-
-            @pl.when(zl == NZ - 1)
-            def _():
-                out_g[...] = (total + z_flow[0, zl].astype(F32)).astype(BF)
-
-            @pl.when((zl > 0) & (zl < NZ - 1))
-            def _():
-                out_g[...] = (total + z_flow[0, zl].astype(F32) + z_flow[1, zl].astype(F32)).astype(BF)
+                    grad[y, d] = (grad[y, d].astype(F32) + z_flow[way, d].astype(F32)).astype(BF)
+
+            if e:
+                gz_copy(d, side).start()
+            else:
+                gz_copy(d, 2).wait_recv()
+                out_g[...] = (grad[y, d].astype(F32) + z_flow[2, 0].astype(F32)).astype(BF)
 
     for j in range(CH):
         zs_arrival(2, j).wait_recv()
@@ -659,16 +674,15 @@
         pltpu.VMEM((3, CH, 2, OWN, CW), BF),
         pltpu.VMEM(blocks, BF),
         pltpu.VMEM(blocks, BF),
-        pltpu.VMEM(blocks, BF),
         pltpu.VMEM((NY, NZ, ROWS, 4 * HD), BF),
         pltpu.VMEM((2, NZ, HALF, 4 * HD), BF),
         pltpu.VMEM((2, NZ, ROWS, 4 * HD), BF),
-        pltpu.VMEM((2, NZ, ROWS, 4 * HD), BF),
+        pltpu.VMEM((3, NZ, ROWS, 4 * HD), BF),
         dma((2 * CH + 4,)),
-        dma((2, NZ, 2)),
+        dma((2, NZ, 3)),
         dma((2, NZ)),
-        dma((2, NZ, 2)),
-        dma((2, NZ, 2)),
+        dma((2, NZ, 2, 2)),
+        dma((2, NZ, 2, 2)),
         dma((2, NZ, 2)),
         dma((2, NZ, 2)),
         dma((3, CH)),
@@ -686,7 +700,7 @@
         dma((2, NZ)),
         dma((2, NZ)),
         dma((NZ,)),
-        dma((2, NZ)),
+        dma((3, NZ)),
     ]
     out_v, out_g = pl.pallas_call(
         kernel,

time: 195 us -> 178 us (0.913)
  the two profiles are of different devices: /device:TPU:66 before, /device:TPU:64 now
where the time goes in v2:
time: 178 us
  Pallas kernels  174 us (98%)
  local copies, waits for them, and re-layouts  3.08 us (2%)
    pallas_call x1, Pallas kernels, on_device(): pl.pallas_call(kernel, name='distill_step', out_shape=(jax.ShapeDtypeStru...  174 us

profile of v2, /device:TPU:64, one launch (start us, length us, event | category | flops | bytes accessed | tf_op | source)
XLA Modules:
  0.0 178.1 jit_solution(16935901086945782975)
XLA Ops:
  1.3 173.7 %distill_step.1 = (bf16[16,3072]{1,0:T(8,128)(2,1)}, bf16[96,512]{1,0:T(8,128)(2,1)}) custom-call(s32[1]{0:T(128)S(6)} %copy.11.time_ref, bf16[256,3072]{1,0:T(8,128)(2,1)} %bitcast.4, bf16[256,3072]{1,0:T(8,128)(2,1)} %bitcast.5, bf16[96,512]{1,0:T(8,128)(2,1)} %wt_hbm.1, bf16[96,512]{1,0:T(8,128)(2,1)} %ws_hbm.1, bf16[256,128]{1,0:T(8,128)(2,1)} %tt_hbm.1, ...), custom_call_target="tpu_custom_call" | custom-call | flops 4000000000 | bytes 4000000 | tf_op jit(solution)/shard_map/distill_step/pallas_call | solution.py:705
  175.0 1.5 copy.12
  176.5 1.5 copy.13

commit v3 on v2

--- a/solution.py
+++ b/solution.py
@@ -147,7 +147,6 @@
     partners = [far_dev, z_to(NG), z_to(1), z_to(-1), x_to(2), y_to(1), y_to(-1), x_to(1), x_to(3), core_dev]
     for device in partners:
         pl.semaphore_signal(barrier, inc=1, device_id=device, device_id_type=MESH)
-    pl.semaphore_wait(barrier, len(partners))
 
     inner_r, inner_l = zl < NZ - 1, zl > 0
     events = [
@@ -236,15 +235,21 @@
                 wy_arrival(m, o, way, way).wait_recv()
                 wh_copy(m, o, way).start()
 
-    def w_hwait(m):
+    def w_near(m):
         def body(o, carry):
             for way in range(2):
                 wy_arrival(m, o, way, 1 - way).wait_recv()
+            return carry
+
+        lax.fori_loop(0, NZ, body, 0)
+
+    def w_far(m):
+        def body(o, carry):
+            for way in range(2):
                 wh_arrival(m, o, way).wait_recv()
             return carry
 
         lax.fori_loop(0, NZ, body, 0)
-        own_w[m].wait()
 
     def w_drain(m):
         wz_copy(m, zl, 2).wait_send()
@@ -340,16 +345,19 @@
                 for k in range(NX):
                     ac_copy(n, shared, j, k, c).wait_send()
 
-    def project(src, m):
-        acc[...] = jnp.zeros_like(acc)
-
-        @pl.loop(0, CH)
-        def _(j):
-            left = src[j].reshape(SEQ, CW)
-            right = w[m, pl.ds(NZ * j, NZ), :, 0 : 3 * HD].reshape(CW, 3 * HD)
-            acc[...] += mm(left, right)
-
-        return acc[...].astype(BF)
+    def project(m, k):
+        j = (y + k) % NY
+        right = w[m, pl.ds(NZ * j, NZ), :, 0 : 3 * HD].reshape(CW, 3 * HD)
+        part = mm(normed[j].reshape(SEQ, CW), right)
+        acc[...] = part if k == 0 else acc[...] + part
+
+    def project_rest(m):
+        w_near(m)
+        project(m, 1)
+        project(m, 3)
+        w_far(m)
+        project(m, 2)
+        proj[...] = acc[...].astype(BF)
 
     scale = HD ** (-0.5)
 
@@ -369,10 +377,6 @@
 
     shape6 = (2, NX, 2, OWN, CW)
 
-    w_zstep(0, 0)
-
-    for e in range(1, 4):
-        w_zstep(0, e)
     for copy in loads[2 * CH :]:
         copy.wait()
     steps = jnp.full((1, CW), time_ref[0].astype(F32))
@@ -391,6 +395,10 @@
         if m == 1:
             gates[pl.ds(2, 1)] = jnp.sum(frequency * (cos_p * high - sin_p * low), axis=0, keepdims=True)
 
+    pl.semaphore_wait(barrier, len(partners))
+    w_zstep(0, 0)
+    for e in range(1, 4):
+        w_zstep(0, e)
     for e in range(4, 8):
         w_zstep(0, e)
     for e in (0, 1, 2):
@@ -425,14 +433,15 @@
         w_zstep(0, e)
     w_zstep(1, 0, False)
     mix_rows(11, 16)
+    own_w[0].wait()
+    project(0, 0)
     for e in (6, 7, 8, 9, 10, 11, 12, 13):
         w_ystep(0, e)
-    w_hwait(0)
+    project_rest(0)
     wy_later(1, 0)
     for e in (1, 2, 3):
         w_zstep(1, e)
 
-    proj[...] = project(normed, 0)
     attend(0)
     for j in range(CH):
         term[j] = mm_t(gated[...], out_columns(0, j)).astype(BF).reshape(shape6)
@@ -457,6 +466,8 @@
         w_zstep(1, e)
     for e in (0, 1, 2, 3, 4, 5, 6, 7):
         w_ystep(1, e)
+    own_w[1].wait()
+    project(1, 0)
     velocity_rows(0)
     for e in (8, 9, 10, 11):
         w_ystep(1, e)
@@ -468,8 +479,7 @@
     share_forward(0, vel, 1)
     velocity_rows(3)
     share_forward(0, vel, 2)
-    w_hwait(1)
-    proj[...] = project(normed, 1)
+    project_rest(1)
 
     attend(1)
     share_forward(0, vel, 3)
@@ -517,6 +527,9 @@
         sum_z_start(1, j)
     for j in range(CH):
         sum_x_start(2, s_term, j)
+    w_drain(0)
+    w_drain(1)
+    sum_drain(0, term, vel)
     gap_rows(0)
     gap_rows(1)
     share_forward(1, gap, 0)
@@ -602,6 +615,8 @@
         def _():
             y_second(events[e][0])
 
+    sum_drain(1, g_term, gap)
+
     for e in late_first:
         d, there, side, right, left = events[e]
 
@@ -623,16 +638,12 @@
                 gz_copy(d, 2).wait_recv()
                 out_g[...] = (grad[y, d].astype(F32) + z_flow[2, 0].astype(F32)).astype(BF)
 
+    sum_drain(2, s_term, None)
     for j in range(CH):
         zs_arrival(2, j).wait_recv()
         total = z_sum[2, j, zh].astype(F32) + z_in[2, j, 1 - zh].astype(F32)
         out_v[:, j * CW : (j + 1) * CW] = (noisy[j, zh, x, c] + total).astype(BF)
 
-    w_drain(0)
-    w_drain(1)
-    sum_drain(0, term, vel)
-    sum_drain(1, g_term, gap)
-    sum_drain(2, s_term, None)
 
     @pl.loop(0, NZ)
     def _(d):

time: 178 us -> 178 us (level)
  no operation moved by 1% of the time
where the time goes in v3:
time: 178 us
  Pallas kernels  173 us (97%)
  local copies, waits for them, and re-layouts  3.08 us (2%)
    pallas_call x1, Pallas kernels, on_device(): pl.pallas_call(kernel, name='distill_step', out_shape=(jax.ShapeDtypeStru...  173 us

profile of v3, /device:TPU:64, one launch (start us, length us, event | category | flops | bytes accessed | tf_op | source)
XLA Modules:
  0.0 177.7 jit_solution(16000084270192405425)
XLA Ops:
  1.3 173.3 %distill_step.1 = (bf16[16,3072]{1,0:T(8,128)(2,1)}, bf16[96,512]{1,0:T(8,128)(2,1)}) custom-call(s32[1]{0:T(128)S(6)} %copy.11.time_ref, bf16[256,3072]{1,0:T(8,128)(2,1)} %bitcast.4, bf16[256,3072]{1,0:T(8,128)(2,1)} %bitcast.5, bf16[96,512]{1,0:T(8,128)(2,1)} %wt_hbm.1, bf16[96,512]{1,0:T(8,128)(2,1)} %ws_hbm.1, bf16[256,128]{1,0:T(8,128)(2,1)} %tt_hbm.1, ...), custom_call_target="tpu_custom_call" | custom-call | flops 4000000000 | bytes 4000000 | tf_op jit(solution)/shard_map/distill_step/pallas_call | solution.py:716
  174.6 1.5 copy.12
  176.2 1.5 copy.13
